TPU v7x, 256 devices: a whole 4x4x8 slice. The times are simulated.
256 devices in a mesh: rows: 64 (over z, x, core), cls: 4 (over y).
Axes of the slice: x: 4, y: 4, z: 8, core: 2. Of those that a mesh axis runs over, the one named last changes fastest.
Arguments:
- seed_scores: float32 [1000, 65536], P('cls', 'rows'), may hold values from 0 to 1, as said below
- block_columns: int32 [512, 8], P('rows'), may hold values from 0 to 511, as said below
- affinity: bfloat16 [512, 8, 128, 128], P('rows'), as said below
Outputs:
- pseudo_labels: float32 [1000, 65536], P('cls', 'rows')
Inputs may be any that keep to these rules, and one draw needn't show every extreme that they name: `block_columns`: block row r lists 8 different block columns, each within 4 block rows of r counted cyclically over the 512 block rows; if row r lists column c then row c lists column r. `affinity`: all values are positive, and the block of row r at column c is the transpose of the block of row c at column r, so A is symmetric. `seed_scores`: every node has at most one nonzero entry, which is positive; every class has at least one labelled node.
All inputs are finite; a program needn't handle non-finite values.
Results may differ from a plain program's by a relative error of at most 0.0034.
Values may be sent and summed in bfloat16 or wider, within the bound.
A program may use at most 64 MiB of HBM per device.

v0:
```python
import jax
import jax.numpy as jnp
from jax import lax
from jax.sharding import PartitionSpec as P

BAND = 4
NNZB = 8
ITERS = 3


damping = 0.99
epsilon = 1e-06


def extended_2(x, sides, width):
    for axis, dim in sides:
        count, length = (lax.axis_size(axis), x.shape[dim])
        up = [(i, (i + 1) % count) for i in range(count)]
        down = [(j, i) for i, j in up]
        last = lax.slice_in_dim(x, length - width, length, axis=dim)
        leading = lax.slice_in_dim(x, 0, width, axis=dim)
        before = lax.ppermute(last, axis, up)
        after = lax.ppermute(leading, axis, down)
        x = jnp.concatenate([before, x, after], axis=dim)
    return x


def class_sum(values):
    return jnp.sum(values, axis=1, keepdims=True)


def shards(seed_scores, block_columns, affinity):
    classes_here, nodes_here = seed_scores.shape
    rows_here = affinity.shape[0]
    block_width = affinity.shape[2]
    total_rows = lax.axis_size("rows") * rows_here
    first_row = lax.axis_index("rows") * rows_here
    local_rows = jnp.arange(rows_here, dtype=jnp.int32)
    offset = (
        block_columns - (first_row + local_rows)[:, None] + total_rows // 2
    ) % total_rows - total_rows // 2
    block_slot = local_rows[:, None] + BAND + offset
    degree = jnp.sum(affinity, axis=(1, 3), dtype=jnp.float32)
    inverse_root = lax.rsqrt(degree).reshape(-1)
    solution = jnp.zeros_like(seed_scores)
    residual = seed_scores
    direction = seed_scores
    norm_now = lax.psum(class_sum(residual * residual), "rows")
    for iteration in range(ITERS):
        scaled = (direction * inverse_root[None, :]).astype(jnp.bfloat16)
        scaled = scaled.reshape(classes_here, rows_here, block_width)
        propagate_extended = extended_2(scaled, (("rows", 1),), BAND)
        picked = jnp.take(propagate_extended, block_slot.reshape(-1), axis=1)
        picked = picked.reshape(classes_here, rows_here, NNZB, block_width)
        summed = jnp.einsum("ljab,cljb->cla", affinity, picked, preferred_element_type=jnp.float32)
        mapped = direction - damping * inverse_root[None, :] * summed.reshape(
            classes_here, nodes_here
        )
        step_size = norm_now / lax.psum(class_sum(direction * mapped), "rows")
        solution = solution + step_size * direction
        residual = residual - step_size * mapped
        norm_next = lax.psum(class_sum(residual * residual), "rows")
        direction = residual + norm_next / norm_now * direction
        norm_now = norm_next
    strength = lax.psum(jnp.sum(solution * solution, axis=0), "cls")
    return solution * lax.rsqrt(strength + epsilon)[None, :]


def solution(mesh):
    return jax.shard_map(
        shards,
        mesh=mesh,
        in_specs=(P("cls", "rows"), P("rows", None), P("rows", None, None, None)),
        out_specs=P("cls", "rows"),
        check_vma=False,
    )
```

profile of v0, /device:TPU:2, one launch (start us, length us, event | category | flops | bytes accessed | tf_op | source)
XLA Modules:
  0.0 727.8 jit_solution(14310658340666947479)
XLA Ops:
  0.0 0.0 copy-start.6
  0.0 1.9 convert_reduce_fusion
  2.0 1.3 multiply_convert_fusion.2
  3.3 0.2 copy.13
  3.5 0.3 copy.14
  3.8 0.1 collective-permute-start
  3.9 1.7 collective-permute-start.1
  5.7 0.0 copy-done.6
  5.7 0.1 fusion.3
  5.7 0.1 reshape.61
  5.9 3.8 collective-permute-done
  9.7 0.0 collective-permute-done.1
  9.7 0.1 pad_maximum_fusion
  9.8 3.0 gather_fusion
  12.8 0.0 copy-start.1
  12.8 2.8 broadcast_select_fusion.2
  15.6 0.1 copy-done.1
  15.7 0.0 copy-start
  15.7 1.5 fusion.7
  17.2 0.3 copy.17
  17.5 0.0 copy-done
  17.5 0.3 multiply_reduce_fusion.4
  17.8 129.9 %all-reduce = (f32[250,1]{0,1:T(1,128)S(1)}, f32[250,1]{0,1:T(1,128)S(1)}) all-reduce(f32[250,1]{0,1:T(1,128)S(1)} %bitcast.70, f32[250,1]{0,1:T(1,128)S(1)} %bitcast.69), channel_id=1, replica_groups=mesh['rows'=64,'cls'=4] {'rows'}, use_global_device_ids=true, to_apply=%region_1.2 | all-reduce | flops 500 | bytes 4000 | tf_op jit(solution)/shard_map/psum | solution.py:48
  147.7 0.4 multiply_reduce_fusion.3
  148.1 124.1 %psum.51 = f32[250,1]{0,1:T(1,128)S(1)} all-reduce(f32[250,1]{0,1:T(1,128)S(1)} %bitcast.71), channel_id=1, replica_groups=mesh['rows'=64,'cls'=4] {'rows'}, use_global_device_ids=true, to_apply=%region_6.8 | all-reduce | flops 250 | bytes 2000 | tf_op jit(solution)/shard_map/psum | solution.py:62
  272.2 1.2 multiply_convert_fusion.1
  273.3 2.0 copy.18
  275.4 2.1 copy.19
  277.4 1.1 fusion.5
  278.5 0.1 collective-permute-start.2
  278.6 5.1 collective-permute-start.3
  283.7 4.0 collective-permute-done.2
  287.7 0.0 collective-permute-done.3
  287.7 2.1 pad_maximum_fusion.1
  289.8 4.2 gather_fusion.1
  294.0 2.8 broadcast_select_fusion.1
  296.8 0.1 copy-done.2
  296.9 2.4 fusion.8
  299.3 2.5 copy.22
  301.9 1.4 multiply_reduce_fusion.2
  303.3 129.1 %psum.52 = f32[250,1]{0,1:T(1,128)S(1)} all-reduce(f32[250,1]{0,1:T(1,128)S(1)} %bitcast.75), channel_id=1, replica_groups=mesh['rows'=64,'cls'=4] {'rows'}, use_global_device_ids=true, to_apply=%region_8.10 | all-reduce | flops 250 | bytes 2000 | tf_op jit(solution)/shard_map/psum | solution.py:59
  432.5 2.7 multiply_reduce_fusion.1
  435.2 124.0 %psum.53 = f32[250,1]{0,1:T(1,128)S(1)} all-reduce(f32[250,1]{0,1:T(1,128)S(1)} %bitcast.73), channel_id=1, replica_groups=mesh['rows'=64,'cls'=4] {'rows'}, use_global_device_ids=true, to_apply=%region_10.12 | all-reduce | flops 250 | bytes 2000 | tf_op jit(solution)/shard_map/psum | solution.py:62
  559.2 1.4 multiply_convert_fusion
  560.6 0.2 copy.23
  560.9 0.3 copy.24
  561.1 0.0 copy-start.5
  561.2 0.3 collective-permute-start.4
  561.5 5.1 collective-permute-start.5
  566.6 4.0 collective-permute-done.4
  570.6 0.0 copy-done.5
  570.6 0.0 collective-permute-done.5
  570.6 1.2 pad_maximum_fusion.2
  571.7 3.0 gather_fusion.2
  574.7 2.8 broadcast_select_fusion
  577.5 0.1 copy-done.3
  577.6 2.5 fusion.9
  580.1 2.6 copy.27
  582.7 0.0 copy-done.4
  582.7 1.6 fusion
  584.2 129.1 %psum.54 = f32[250,1]{0,1:T(1,128)S(1)} all-reduce(f32[250,1]{0,1:T(1,128)S(1)} %bitcast.74), channel_id=1, replica_groups=mesh['rows'=64,'cls'=4] {'rows'}, use_global_device_ids=true, to_apply=%region_12.14 | all-reduce | flops 250 | bytes 2000 | tf_op jit(solution)/shard_map/psum | solution.py:59
  713.3 1.4 multiply_reduce_fusion
  714.7 10.7 %psum.55 = f32[1024]{0:T(1024)S(1)} all-reduce(f32[1024]{0:T(1024)S(1)} %get-tuple-element.10), channel_id=1, replica_groups=mesh['rows'=64,'cls'=4] {'cls'}, use_global_device_ids=true, to_apply=%region_14.16 | all-reduce | flops 1024 | bytes 8192 | tf_op jit(solution)/shard_map/psum | solution.py:65
  725.4 2.3 broadcast_multiply_fusion
  (17 shorter events, 0.2 us)
Async XLA Ops:
  0.0 5.7 copy-start.6
  3.8 5.9 collective-permute-start
  3.9 5.8 collective-permute-start.1
  12.8 2.9 copy-start.1
  15.7 1.8 copy-start
  278.5 9.2 %collective-permute-start.2 = (bf16[250,4,128]{2,0,1:T(8,128)(2,1)S(1)}, bf16[250,4,128]{2,0,1:T(8,128)(2,1)S(1)}, u32[]{:S(2)}, u32[]{:S(2)}) collective-permute-start(bf16[250,4,128]{2,0,1:T(8,128)(2,1)S(1)} %get-tuple-element.18), channel_id=1, source_target_pairs={{0,4},{4,8},{8,12},{12,16},{16,20},{20,24},{24,28},{28,32},{32,36}... | collective-permute-start | bytes 768008 | tf_op jit(solution)/shard_map/ppermute | solution.py:22
  278.6 9.1 %collective-permute-start.3 = (bf16[250,4,128]{2,0,1:T(8,128)(2,1)S(1)}, bf16[250,4,128]{2,0,1:T(8,128)(2,1)S(1)}, u32[]{:S(2)}, u32[]{:S(2)}) collective-permute-start(bf16[250,4,128]{2,0,1:T(8,128)(2,1)S(1)} %get-tuple-element.19), channel_id=1, source_target_pairs={{4,0},{8,4},{12,8},{16,12},{20,16},{24,20},{28,24},{32,28},{36,32}... | collective-permute-start | bytes 768008 | tf_op jit(solution)/shard_map/ppermute | solution.py:23
  294.0 2.9 copy-start.2
  561.1 9.4 %copy-start.5 = (bf16[250,8,128]{2,0,1:T(8,128)(2,1)}, bf16[250,8,128]{2,0,1:T(8,128)(2,1)S(1)}, u32[]{:S(2)}) copy-start(bf16[250,8,128]{2,0,1:T(8,128)(2,1)S(1)} %copy.24) | copy-start | bytes 1536004
  561.2 9.4 %collective-permute-start.4 = (bf16[250,4,128]{2,0,1:T(8,128)(2,1)S(1)}, bf16[250,4,128]{2,0,1:T(8,128)(2,1)S(1)}, u32[]{:S(2)}, u32[]{:S(2)}) collective-permute-start(bf16[250,4,128]{2,0,1:T(8,128)(2,1)S(1)} %get-tuple-element.16), channel_id=1, source_target_pairs={{0,4},{4,8},{8,12},{12,16},{16,20},{20,24},{24,28},{28,32},{32,36}... | collective-permute-start | bytes 768008 | tf_op jit(solution)/shard_map/ppermute | solution.py:22
  561.5 9.1 %collective-permute-start.5 = (bf16[250,4,128]{2,0,1:T(8,128)(2,1)S(1)}, bf16[250,4,128]{2,0,1:T(8,128)(2,1)S(1)}, u32[]{:S(2)}, u32[]{:S(2)}) collective-permute-start(bf16[250,4,128]{2,0,1:T(8,128)(2,1)S(1)} %get-tuple-element.17), channel_id=1, source_target_pairs={{4,0},{8,4},{12,8},{16,12},{20,16},{24,20},{28,24},{32,28},{36,32}... | collective-permute-start | bytes 768008 | tf_op jit(solution)/shard_map/ppermute | solution.py:23
  574.7 2.9 copy-start.3
  577.6 5.1 copy-start.4
where the time goes:
time: 732 us; the launch traced here: 728 us
  blocking collectives  647 us (88%)
  other arithmetic  27.9 us (4%)
  local copies, waits for them, and re-layouts  22.2 us (3%)
  starting transfers between devices  12.4 us (2%)
  waiting for transfers between devices  11.8 us (2%)
    psum x2, blocking collectives, shards(): step_size = norm_now / lax.psum(class_sum(direction * mapped), 'rows')  258 us
    psum x2, blocking collectives, shards(): norm_next = lax.psum(class_sum(residual * residual), 'rows')  248 us
    psum x1, blocking collectives, shards(): norm_now = lax.psum(class_sum(residual * residual), 'rows')  130 us
  transfers between devices with their start and end apart: 6, of which 3 were waited for; matrix products, arithmetic and copies ran while one was open for 0% of the time, Pallas kernels for 0%

commit v1 on v0

v1 whole, which is shorter than its diff:
```python
import functools

import jax
import jax.numpy as jnp
from jax import lax
from jax.experimental import pallas as pl
from jax.experimental.pallas import tpu as pltpu
from jax.sharding import PartitionSpec as P

MESH = pl.DeviceIdType.MESH
BAND = 4
NNZB = 8
BLK = 128
WIDE = 256
GROUP = 8
VMEM_BYTES = 527 * 1024 * 1024 // 10
damping = 0.99
epsilon = 1e-06
F32 = jnp.float32
BF16 = jnp.bfloat16


def column(table, index, width):
    return jnp.broadcast_to(table[:, index : index + 1], (BLK, width))


def node_sum(x):
    return jnp.sum(x, axis=0, keepdims=True)


def ratio(top, bottom):
    good = (bottom > 0) & (top > 0)
    return jnp.where(good, top / jnp.where(good, bottom, 1.0), 0.0)


def combination(early, middle, q):
    g00, g01, g11 = early
    g02, g12, g22 = middle
    g = damping
    gram = [[g00, g01, g02, g12], [g01, g11, g12, g22], [g02, g12, g22, q]]

    def square(p):
        return sum(p[i] * p[j] * gram[i][j] for i in range(len(p)) for j in range(len(p)))

    def energy(p):
        return sum(
            p[i] * p[j] * (gram[i][j] - g * gram[i][j + 1])
            for i in range(len(p))
            for j in range(len(p))
        )

    a0 = ratio(g00, g00 - g * g01)
    r1 = [1.0 - a0, g * a0]
    rr1 = square(r1)
    b0 = ratio(rr1, g00)
    d1 = [r1[0] + b0, r1[1]]
    a1 = ratio(rr1, energy(d1))
    r2 = [r1[0] - a1 * d1[0], r1[1] - a1 * (d1[1] - g * d1[0]), a1 * g * d1[1]]
    rr2 = square(r2)
    b1 = ratio(rr2, rr1)
    d2 = [r2[0] + b1 * d1[0], r2[1] + b1 * d1[1], r2[2]]
    a2 = ratio(rr2, energy(d2))
    return a0 + a1 * d1[0] + a2 * d2[0], a1 * d1[1] + a2 * d2[1], a2 * d2[2]


OWN = {i: (max(i, 2), min(i + 4, 5)) for i in range(4)}
HALO = {0: (0, 1), 1: (1, 1), 2: (6, 6), 3: (6, 7)}
OUTER = (0, 1, 6, 7)
TILES = ((0, 0), (0, 1), (1, 1), (2, 6), (3, 6), (3, 7))


def kernel(
    n_rows, n_cls,
    seed_hbm, columns_hbm, affinity_hbm, result,
    columns_ref, seed, raw, band, across, field1, field2a, field2b, field3a, field3b, v0, v1, v2, root, self_part, outer_root, outer_v0, outer_self,
    reach, turned1, turned2,
    code_out, code_left, code_right, apart_out, apart_left, apart_right, first_out, first_in, second_out, second_in,
    part_a, part_b, part_all, got_a, got_b, got_all, strength_out, strength_in,
    load_sem, halo_send, halo_recv, sum_send, sum_recv, cls_send, cls_recv, relay_sem,
):
    me = lax.axis_index("rows")
    mine = lax.axis_index("cls")
    low, high = lax.rem(me, GROUP), me // GROUP
    n_high = n_rows // GROUP
    total_blocks = n_rows * 8

    columns_copy = pltpu.make_async_copy(columns_hbm, columns_ref, load_sem.at[9])
    columns_copy.start()
    seed_copy = pltpu.make_async_copy(seed_hbm, seed, load_sem.at[8])
    seed_copy.start()
    raw_copies = []
    for r in range(8):
        copy = pltpu.make_async_copy(affinity_hbm.at[r], raw.at[r], load_sem.at[r])
        copy.start()
        raw_copies.append(copy)

    left = {"rows": lax.rem(me + n_rows - 1, n_rows), "cls": mine}
    right = {"rows": lax.rem(me + 1, n_rows), "cls": mine}
    far = sorted(range(1, GROUP), key=lambda d: -min(d, GROUP - d))
    peers_a = [{"rows": high * GROUP + lax.rem(low + d, GROUP), "cls": mine} for d in far]
    far = sorted(range(1, n_high), key=lambda d: -min(d, n_high - d))
    peers_b = [{"rows": lax.rem(high + d, n_high) * GROUP + low, "cls": mine} for d in far]
    far = sorted(range(1, n_cls), key=lambda d: -min(d, n_cls - d))
    peers_c = [{"rows": me, "cls": lax.rem(mine + d, n_cls)} for d in far]
    barrier = pltpu.get_barrier_semaphore()
    above = {"rows": lax.rem(high + 1, n_high) * GROUP + low, "cls": mine}
    below = {"rows": lax.rem(high + n_high - 1, n_high) * GROUP + low, "cls": mine}
    later = list(range(1, n_high)) + [0]
    peers_all = [
        {"rows": lax.rem(high + dz, n_high) * GROUP + lax.rem(low + d, GROUP), "cls": mine}
        for dz in later
        for d in range(GROUP)
        if (dz, d) != (0, 0)
    ]
    partners = [left, right] + [above, below] + peers_a + peers_c
    for device in partners:
        pl.semaphore_signal(barrier, inc=1, device_id=device, device_id_type=MESH)

    sent = []

    def send(source, target, send_sem, recv_sem, device):
        copy = pltpu.make_async_remote_copy(
            src_ref=source, dst_ref=target, send_sem=send_sem, recv_sem=recv_sem,
            device_id=device, device_id_type=MESH,
        )
        copy.start()
        sent.append(copy)
        return copy

    def packed(sums):
        pieces = [half for x in sums for half in (x[:, :BLK], x[:, BLK:])]
        if len(pieces) < 8:
            pieces.append(jnp.zeros((8 - len(pieces), BLK), F32))
        return jnp.concatenate(pieces, axis=0)

    def scatter(tile, out, got, peers, send_sem, recv_sem):
        out[...] = tile
        for d, device in enumerate(peers):
            copy = pltpu.make_async_remote_copy(
                src_ref=out, dst_ref=got.at[d], send_sem=send_sem, recv_sem=recv_sem,
                device_id=device, device_id_type=MESH,
            )
            copy.start()
        if peers:
            scattered.append((got, send_sem))
        return tile, got, peers, recv_sem

    def gather(tile, got, peers, recv_sem):
        if peers:
            pltpu.make_async_copy(got, got, recv_sem).wait()
            tile = tile + jnp.sum(got[...], axis=0)
        return tile

    scattered = []

    n_relays = n_high // 2

    def relay(step):
        if 0 < step <= n_relays:
            pl.semaphore_wait(relay_sem.at[step - 1], 2)
        if step < n_relays:
            for device in (above, below):
                pl.semaphore_signal(relay_sem.at[step], inc=1, device_id=device, device_id_type=MESH)

    lane = lax.broadcasted_iota(jnp.int32, (BLK, BLK), 1)
    diagonal = lane == lax.broadcasted_iota(jnp.int32, (BLK, BLK), 0)
    wide_lane = lax.broadcasted_iota(jnp.int32, (BLK, WIDE), 1).astype(F32)
    columns_copy.wait()
    places = []
    for r in range(8):
        offsets = [
            lax.rem(columns_ref[r, j] - (me * 8 + r) + BAND + total_blocks, total_blocks) for j in range(NNZB)
        ]
        absent = sum(range(9)) - sum(offsets)
        slots = []
        for o in range(9):
            j = 0
            for i in range(1, NNZB):
                j = jnp.where(offsets[i] == o, i, j)
            slots.append((j, (absent != o).astype(F32)))
        places.append(slots)

    seed_copy.wait()
    scores = seed[...]
    class_id = lax.broadcasted_iota(jnp.int32, scores.shape, 0).astype(F32)
    value = node_sum(scores)
    label = node_sum(jnp.where(scores > 0, class_id, 0.0))
    rows = [value[:, BLK * r : BLK * (r + 1)] for r in range(8)]
    rows += [label[:, BLK * r : BLK * (r + 1)] for r in range(8)]
    rows = jnp.concatenate(rows, axis=0)
    code_out[:16] = rows
    code = jnp.concatenate([rows, jnp.zeros((BLK - 16, BLK), F32)], axis=0).T
    for r in range(8):
        v0[BLK * r : BLK * (r + 1)] = jnp.where(
            column(code, 8 + r, WIDE) == wide_lane, column(code, r, WIDE), 0.0
        )

    inverses = jnp.zeros((BLK, BLK), F32)
    for r in range(8):
        raw_copies[r].wait()
        degree = jnp.sum(jnp.sum(raw[r].astype(F32), axis=0), axis=1, keepdims=True)
        inverse = lax.rsqrt(degree)
        root[BLK * r : BLK * (r + 1)] = jnp.broadcast_to(inverse, (BLK, WIDE))
        inverses = jnp.where(lane == r, inverse, inverses)
    code_out[16:] = inverses.T[:8]

    pl.semaphore_wait(barrier, len(partners))
    to_left = send(code_out, code_right, halo_send.at[0], halo_recv.at[0], left)
    to_right = send(code_out, code_left, halo_send.at[1], halo_recv.at[1], right)
    relay(0)

    def fill(r):
        half = r % 2
        row = pl.ds(BLK * half, BLK)
        apart = None
        for o in range(9):
            slot, present = places[r][o]
            block = raw[r, slot] * present.astype(BF16)
            if o == BAND:
                block = block.astype(F32)
                inverse = root[BLK * r : BLK * (r + 1), :BLK]
                apart = jnp.sum(jnp.where(diagonal, block, 0.0), axis=1, keepdims=True) * inverse * inverse
                self_part[BLK * r : BLK * (r + 1)] = jnp.concatenate([apart, apart], axis=1)
                block = jnp.where(diagonal, 0.0, block).astype(BF16)
            band[r // 2, row, BLK * (o + half) : BLK * (o + half + 1)] = block
        blank = 9 if half == 0 else 0
        band[r // 2, row, BLK * blank : BLK * (blank + 1)] = jnp.zeros((BLK, BLK), BF16)
        return apart

    def part(i, fields, pairs):
        first, last = pairs
        block = band[i, :, WIDE * (first - i) : WIDE * (last + 1 - i)]
        return sum(
            jnp.dot(block, field[WIDE * first : WIDE * (last + 1)], preferred_element_type=F32) for field in fields
        )

    def split(fields, rows, x):
        high = x.astype(BF16)
        fields[0][rows] = high
        fields[1][rows] = (x - high.astype(F32)).astype(BF16)

    field2, field3 = (field2a, field2b), (field3a, field3b)

    def pair(ref, i):
        return ref.at[pl.ds(WIDE * i, WIDE)]

    def own(fields, i):
        return pair(root, i)[...] * part(i, fields, OWN[i])

    def outward(fields, k, pairs=range(4)):
        return sum(
            jnp.dot(across[t], field[WIDE * (i + 2) : WIDE * (i + 3)], preferred_element_type=F32)
            for t, (i, at) in enumerate(TILES)
            if at == k and i in pairs
            for field in fields
        )

    for r in range(8):
        rows = pl.ds(BLK * r, BLK)
        field1[512 + BLK * r : 512 + BLK * (r + 1)] = (root[rows] * v0[rows]).astype(BF16)
    first = {}
    aparts = jnp.zeros((BLK, BLK), F32)
    for i in (0, 3, 1, 2):
        for r in (2 * i, 2 * i + 1):
            aparts = jnp.where(lane == r, fill(r), aparts)
        partial = own((field1,), i)
        first_out[i] = partial.astype(BF16)
        target, device = (first_in.at[2 + i], left) if i < 2 else (first_in.at[i - 2], right)
        first[i] = send(first_out.at[i], target, halo_send.at[2 + i], halo_recv.at[2 + i], device)
        pair(v1, i)[...] = partial + pair(self_part, i)[...] * pair(v0, i)[...]
    apart_out[...] = aparts.T[:8]
    aparts_left = send(apart_out, apart_right, halo_send.at[8], halo_recv.at[8], left)
    aparts_right = send(apart_out, apart_left, halo_send.at[9], halo_recv.at[9], right)
    relay(1)
    for t, (i, k) in enumerate(TILES):
        across[t] = band[i, :, WIDE * (k - i) : WIDE * (k - i + 1)].T
    for h, k in enumerate(OUTER):
        reach[h] = outward((field1,), k)

    to_left.wait_recv()
    to_right.wait_recv()
    outer = jnp.concatenate([code_left[...], code_right[...], jnp.zeros((BLK - 48, BLK), F32)], axis=0).T
    for e in range(4):
        for at, h, base in ((e, e // 2, 4 + e), (12 + e, 2 + e // 2, 24 + e)):
            rows = pl.ds(BLK * (e % 2), BLK)
            here = jnp.where(column(outer, base + 8, WIDE) == wide_lane, column(outer, base, WIDE), 0.0)
            inverse = column(outer, base + 16, WIDE)
            field1[BLK * at : BLK * (at + 1)] = (inverse * here).astype(BF16)
            outer_root[h, rows] = inverse
            outer_v0[h, rows] = here
    for i in range(4):
        inverse = pair(root, i)[...]
        after = pair(v1, i)[...] + inverse * part(i, (field1,), HALO[i])
        pair(v1, i)[...] = after
        split(field2, pl.ds(512 + WIDE * i, WIDE), inverse * after)

    second = []
    for n, i in enumerate((0, 3)):
        partial = own(field2, i)
        second_out[n] = partial.astype(BF16)
        second.append(
            send(second_out.at[n], second_in.at[1 - n], halo_send.at[6 + n], halo_recv.at[6 + n], (left, right)[n])
        )
        pair(v2, i)[...] = partial + pair(self_part, i)[...] * pair(v1, i)[...]
    relay(2)
    for i in (1, 2):
        pair(v2, i)[...] = own(field2, i) + pair(self_part, i)[...] * pair(v1, i)[...]
    aparts_left.wait_recv()
    aparts_right.wait_recv()
    outer = jnp.concatenate([apart_left[...], apart_right[...], jnp.zeros((BLK - 16, BLK), F32)], axis=0).T
    for e in range(4):
        for h, at in ((e // 2, 4 + e), (2 + e // 2, 8 + e)):
            rows = pl.ds(BLK * (e % 2), BLK)
            apart = column(outer, at, WIDE)
            outer_self[h, rows] = apart
            reach[h, rows] = outer_root[h, rows] * reach[h, rows] + apart * outer_v0[h, rows]
    early = [node_sum(v0[...] * v0[...]), node_sum(v0[...] * v1[...]), node_sum(v1[...] * v1[...])]
    early = scatter(packed(early), part_a, got_a, peers_a, sum_send.at[0], sum_recv.at[0])
    for r in range(8):
        turned1[:, BLK * r : BLK * (r + 1)] = v1[BLK * r : BLK * (r + 1)].T

    for i in (3, 2, 0, 1):
        first[i].wait_recv()
    for h, k in enumerate(OUTER):
        after = first_in[h].astype(F32) + reach[h]
        reach[h] = after
        split(field2, pl.ds(WIDE * k, WIDE), outer_root[h] * after)
    for i in range(4):
        inverse = pair(root, i)[...]
        after = pair(v2, i)[...] + inverse * part(i, field2, HALO[i])
        pair(v2, i)[...] = after
        split(field3, pl.ds(512 + WIDE * i, WIDE), inverse * after)
    sums = [node_sum(v0[...] * v2[...]), node_sum(v1[...] * v2[...]), node_sum(v2[...] * v2[...])]

    relay(3)
    early = scatter(gather(*early), part_b, got_b, peers_b, sum_send.at[1], sum_recv.at[1])

    form = jnp.zeros((1, WIDE), F32)
    for i in range(4):
        field = pair(v2, i)[...]
        form = form + node_sum(field * (own(field3, i) + pair(self_part, i)[...] * field))
    for n, (h, k, pairs) in enumerate(((1, 1, (1,)), (2, 6, (2, 3)))):
        inverse = outer_root[h]
        weight = 2.0 * inverse * outward(field3, k, pairs)
        form = form + node_sum(weight * (inverse * outward(field2, k) + outer_self[h] * reach[h]))
        reach[3 * n] = weight
    for r in range(8):
        turned2[:, BLK * r : BLK * (r + 1)] = v2[BLK * r : BLK * (r + 1)].T
    for n in range(2):
        second[1 - n].wait_recv()
        form = form + node_sum(second_in[n].astype(F32) * reach[3 * n])
    sums.append(form)

    for step in range(4, n_relays + 1):
        relay(step)
    late = scatter(packed(sums), part_all, got_all, peers_all, sum_send.at[2], sum_recv.at[2])
    early = gather(*early)
    late = gather(*late)
    grams = [early[2 * i : 2 * i + 2] for i in range(3)] + [late[2 * i : 2 * i + 2] for i in range(4)]
    weights = combination(grams[:3], grams[3:6], grams[6])
    weights = jnp.concatenate(list(weights) + [jnp.zeros((BLK - 6, BLK), F32)], axis=0).T
    n_classes = seed.shape[0]
    columns = [
        jnp.concatenate([weights[:, 2 * i : 2 * i + 1], weights[:, 2 * i + 1 : 2 * i + 2]], axis=0)[:n_classes]
        for i in range(3)
    ]
    n_lanes = seed.shape[1]
    strength = jnp.zeros((8, n_lanes), F32)
    for at in range(0, n_classes, 8):
        here = slice(at, min(at + 8, n_classes))
        c0, c1, c2 = (jnp.broadcast_to(c[here], (here.stop - at, n_lanes)) for c in columns)
        x = c0 * seed[here] + c1 * turned1[here] + c2 * turned2[here]
        result[here] = x
        if here.stop - at == 8:
            strength = strength + x * x
        else:
            rest = node_sum(x * x)
    strength = node_sum(strength)
    if n_classes % 8:
        strength = strength + rest
    strength = jnp.concatenate([strength[:, BLK * r : BLK * (r + 1)] for r in range(8)], axis=0)
    strength = gather(*scatter(strength, strength_out, strength_in, peers_c, cls_send, cls_recv))
    norm = lax.rsqrt(strength + epsilon)
    for r in range(8):
        here = pl.ds(BLK * r, BLK)
        result[:, here] = result[:, here] * norm[r : r + 1]
    for copy in sent:
        copy.wait_send()
    for got, send_sem in scattered:
        pltpu.make_async_copy(got, got, send_sem).wait()


def shards(n_rows, n_cls, seed_scores, block_columns, affinity):
    n_classes, n_nodes = seed_scores.shape
    n_high = n_rows // GROUP
    field = pltpu.VMEM((2048, WIDE), BF16)
    whole = pltpu.VMEM((1024, WIDE), F32)
    turned = pltpu.VMEM((WIDE, 1024), F32)
    code = pltpu.VMEM((24, BLK), F32)
    tile = pltpu.VMEM((8, BLK), F32)
    outside = pltpu.VMEM((4, WIDE, WIDE), F32)
    return pl.pallas_call(
        functools.partial(kernel, n_rows, n_cls),
        out_shape=jax.ShapeDtypeStruct(seed_scores.shape, F32),
        in_specs=[pl.BlockSpec(memory_space=pl.ANY)] * 3,
        out_specs=pl.BlockSpec(memory_space=pltpu.VMEM),
        scratch_shapes=[
            pltpu.SMEM((8, NNZB), jnp.int32),
            pltpu.VMEM((n_classes, n_nodes), F32),
            pltpu.VMEM((8, NNZB, BLK, BLK), BF16),
            pltpu.VMEM((4, WIDE, 10 * BLK), BF16),
            pltpu.VMEM((len(TILES), WIDE, WIDE), BF16),
            field, field, field, field, field,
            whole, whole, whole, whole, whole,
            outside, outside, outside, outside,
            turned, turned,
            code, code, code, tile, tile, tile,
            pltpu.VMEM((4, WIDE, WIDE), BF16), pltpu.VMEM((4, WIDE, WIDE), BF16),
            pltpu.VMEM((2, WIDE, WIDE), BF16), pltpu.VMEM((2, WIDE, WIDE), BF16),
            tile, tile, tile,
            pltpu.VMEM((GROUP - 1, 8, BLK), F32),
            pltpu.VMEM((max(n_high - 1, 1), 8, BLK), F32),
            pltpu.VMEM((n_rows - 1, 8, BLK), F32),
            tile,
            pltpu.VMEM((max(n_cls - 1, 1), 8, BLK), F32),
            pltpu.SemaphoreType.DMA((10,)),
            pltpu.SemaphoreType.DMA((10,)),
            pltpu.SemaphoreType.DMA((10,)),
            pltpu.SemaphoreType.DMA((3,)),
            pltpu.SemaphoreType.DMA((3,)),
            pltpu.SemaphoreType.DMA,
            pltpu.SemaphoreType.DMA,
            pltpu.SemaphoreType.REGULAR((max(n_high // 2, 1),)),
        ],
        compiler_params=pltpu.CompilerParams(
            collective_id=0, has_side_effects=True, vmem_limit_bytes=VMEM_BYTES
        ),
        cost_estimate=pl.CostEstimate(flops=1600000000, bytes_accessed=4000000, transcendentals=0),
    )(seed_scores, block_columns, affinity)


def solution(mesh):
    return jax.shard_map(
        functools.partial(shards, mesh.shape["rows"], mesh.shape["cls"]),
        mesh=mesh,
        in_specs=(P("cls", "rows"), P("rows", None), P("rows", None, None, None)),
        out_specs=P("cls", "rows"),
        check_vma=False,
    )
```

time: 732 us -> 38.4 us (0.05)
  the two profiles are of different devices: /device:TPU:2 before, /device:TPU:1 now
where the time goes in v1:
time: 38.4 us; the launch traced here: 38.3 us
  Pallas kernels  36.7 us (96%)
  local copies, waits for them, and re-layouts  1.66 us (4%)
    pallas_call x1, Pallas kernels, shards(): pl.pallas_call(functools.partial(kernel, n_rows, n_cls), out_shape=jax.Sh...  36.7 us
    unnamed x3, local copies, waits for them, and re-layouts  1.66 us

profile of v1, /device:TPU:1, one launch (start us, length us, event | category | flops | bytes accessed | tf_op | source)
XLA Modules:
  0.0 38.3 jit_solution(14765562942110900771)
XLA Ops:
  0.0 0.0 copy-start
  0.0 0.7 %copy-done = s32[8,8]{1,0:T(8,128)S(1)} copy-done((s32[8,8]{1,0:T(8,128)S(1)}, s32[8,8]{1,0:T(8,128)}, u32[]{:S(2)}) %copy-start) | copy-done | bytes 280
  0.7 36.7 %shard_map.37 = f32[250,1024]{1,0:T(8,128)S(1)} custom-call(f32[250,1024]{1,0:T(8,128)} %seed_hbm.1, s32[8,8]{1,0:T(8,128)S(1)} %copy-done, bf16[8,8,128,128]{3,2,1,0:T(8,128)(2,1)} %affinity_hbm.1), custom_call_target="tpu_custom_call" | custom-call | flops 1600000000 | bytes 4000000 | tf_op jit(solution)/shard_map/pallas_call | solution.py:402
  37.4 1.0 %copy.5 = f32[250,1024]{1,0:T(8,128)} copy(f32[250,1024]{1,0:T(8,128)S(1)} %shard_map.37) | data formatting | bytes 2048000
Async XLA Ops:
  0.0 0.7 %copy-start = (s32[8,8]{1,0:T(8,128)S(1)}, s32[8,8]{1,0:T(8,128)}, u32[]{:S(2)}) copy-start(s32[8,8]{1,0:T(8,128)} %columns_hbm.1) | copy-start | bytes 772

commit v2 on v1

--- a/solution.py
+++ b/solution.py
@@ -75,7 +75,7 @@
     columns_ref, seed, raw, band, across, field1, field2a, field2b, field3a, field3b, v0, v1, v2, root, self_part, outer_root, outer_v0, outer_self,
     reach, turned1, turned2,
     code_out, code_left, code_right, apart_out, apart_left, apart_right, first_out, first_in, second_out, second_in,
-    part_a, part_b, part_all, got_a, got_b, got_all, strength_out, strength_in,
+    part_a, part_b, got_a, got_b, strength_out, strength_in,
     load_sem, halo_send, halo_recv, sum_send, sum_recv, cls_send, cls_recv, relay_sem,
 ):
     me = lax.axis_index("rows")
@@ -98,20 +98,12 @@
     right = {"rows": lax.rem(me + 1, n_rows), "cls": mine}
     far = sorted(range(1, GROUP), key=lambda d: -min(d, GROUP - d))
     peers_a = [{"rows": high * GROUP + lax.rem(low + d, GROUP), "cls": mine} for d in far]
-    far = sorted(range(1, n_high), key=lambda d: -min(d, n_high - d))
-    peers_b = [{"rows": lax.rem(high + d, n_high) * GROUP + low, "cls": mine} for d in far]
+    peers_b = [{"rows": lax.rem(high + d, n_high) * GROUP + low, "cls": mine} for d in range(1, n_high)]
     far = sorted(range(1, n_cls), key=lambda d: -min(d, n_cls - d))
     peers_c = [{"rows": me, "cls": lax.rem(mine + d, n_cls)} for d in far]
     barrier = pltpu.get_barrier_semaphore()
     above = {"rows": lax.rem(high + 1, n_high) * GROUP + low, "cls": mine}
     below = {"rows": lax.rem(high + n_high - 1, n_high) * GROUP + low, "cls": mine}
-    later = list(range(1, n_high)) + [0]
-    peers_all = [
-        {"rows": lax.rem(high + dz, n_high) * GROUP + lax.rem(low + d, GROUP), "cls": mine}
-        for dz in later
-        for d in range(GROUP)
-        if (dz, d) != (0, 0)
-    ]
     partners = [left, right] + [above, below] + peers_a + peers_c
     for device in partners:
         pl.semaphore_signal(barrier, inc=1, device_id=device, device_id_type=MESH)
@@ -129,8 +121,7 @@
 
     def packed(sums):
         pieces = [half for x in sums for half in (x[:, :BLK], x[:, BLK:])]
-        if len(pieces) < 8:
-            pieces.append(jnp.zeros((8 - len(pieces), BLK), F32))
+        pieces.append(jnp.zeros((16 - len(pieces), BLK), F32))
         return jnp.concatenate(pieces, axis=0)
 
     def scatter(tile, out, got, peers, send_sem, recv_sem):
@@ -153,7 +144,7 @@
 
     scattered = []
 
-    n_relays = n_high // 2
+    n_relays = max(n_high // 2 - 1, 0)
 
     def relay(step):
         if 0 < step <= n_relays:
@@ -292,19 +283,24 @@
         inverse = pair(root, i)[...]
         after = pair(v1, i)[...] + inverse * part(i, (field1,), HALO[i])
         pair(v1, i)[...] = after
-        split(field2, pl.ds(512 + WIDE * i, WIDE), inverse * after)
+        field2a[512 + WIDE * i : 512 + WIDE * (i + 1)] = (inverse * after).astype(BF16)
 
     second = []
     for n, i in enumerate((0, 3)):
-        partial = own(field2, i)
+        partial = own((field2a,), i)
         second_out[n] = partial.astype(BF16)
         second.append(
             send(second_out.at[n], second_in.at[1 - n], halo_send.at[6 + n], halo_recv.at[6 + n], (left, right)[n])
         )
+        pair(v2, i)[...] = partial
+    relay(2)
+    for i in range(4):
+        rows = pl.ds(512 + WIDE * i, WIDE)
+        low_part = pair(root, i)[...] * pair(v1, i)[...] - field2a[rows].astype(F32)
+        field2b[rows] = low_part.astype(BF16)
+    for i in range(4):
+        partial = own((field2b,), i) + pair(v2, i)[...] if i in (0, 3) else own(field2, i)
         pair(v2, i)[...] = partial + pair(self_part, i)[...] * pair(v1, i)[...]
-    relay(2)
-    for i in (1, 2):
-        pair(v2, i)[...] = own(field2, i) + pair(self_part, i)[...] * pair(v1, i)[...]
     aparts_left.wait_recv()
     aparts_right.wait_recv()
     outer = jnp.concatenate([apart_left[...], apart_right[...], jnp.zeros((BLK - 16, BLK), F32)], axis=0).T
@@ -314,26 +310,23 @@
             apart = column(outer, at, WIDE)
             outer_self[h, rows] = apart
             reach[h, rows] = outer_root[h, rows] * reach[h, rows] + apart * outer_v0[h, rows]
-    early = [node_sum(v0[...] * v0[...]), node_sum(v0[...] * v1[...]), node_sum(v1[...] * v1[...])]
-    early = scatter(packed(early), part_a, got_a, peers_a, sum_send.at[0], sum_recv.at[0])
-    for r in range(8):
-        turned1[:, BLK * r : BLK * (r + 1)] = v1[BLK * r : BLK * (r + 1)].T
-
+    sums = [node_sum(v0[...] * v0[...]), node_sum(v0[...] * v1[...]), node_sum(v1[...] * v1[...])]
     for i in (3, 2, 0, 1):
         first[i].wait_recv()
     for h, k in enumerate(OUTER):
         after = first_in[h].astype(F32) + reach[h]
         reach[h] = after
         split(field2, pl.ds(WIDE * k, WIDE), outer_root[h] * after)
+    late = [jnp.zeros((1, WIDE), F32)] * 3
     for i in range(4):
         inverse = pair(root, i)[...]
         after = pair(v2, i)[...] + inverse * part(i, field2, HALO[i])
         pair(v2, i)[...] = after
         split(field3, pl.ds(512 + WIDE * i, WIDE), inverse * after)
-    sums = [node_sum(v0[...] * v2[...]), node_sum(v1[...] * v2[...]), node_sum(v2[...] * v2[...])]
-
-    relay(3)
-    early = scatter(gather(*early), part_b, got_b, peers_b, sum_send.at[1], sum_recv.at[1])
+        late[0] = late[0] + node_sum(pair(v0, i)[...] * after)
+        late[1] = late[1] + node_sum(pair(v1, i)[...] * after)
+        late[2] = late[2] + node_sum(after * after)
+    sums += late
 
     form = jnp.zeros((1, WIDE), F32)
     for i in range(4):
@@ -344,19 +337,21 @@
         weight = 2.0 * inverse * outward(field3, k, pairs)
         form = form + node_sum(weight * (inverse * outward(field2, k) + outer_self[h] * reach[h]))
         reach[3 * n] = weight
-    for r in range(8):
-        turned2[:, BLK * r : BLK * (r + 1)] = v2[BLK * r : BLK * (r + 1)].T
     for n in range(2):
         second[1 - n].wait_recv()
         form = form + node_sum(second_in[n].astype(F32) * reach[3 * n])
     sums.append(form)
 
-    for step in range(4, n_relays + 1):
-        relay(step)
-    late = scatter(packed(sums), part_all, got_all, peers_all, sum_send.at[2], sum_recv.at[2])
-    early = gather(*early)
-    late = gather(*late)
-    grams = [early[2 * i : 2 * i + 2] for i in range(3)] + [late[2 * i : 2 * i + 2] for i in range(4)]
+    tile = scatter(packed(sums), part_a, got_a, peers_a, sum_send.at[0], sum_recv.at[0])
+    for r in range(8):
+        turned1[:, BLK * r : BLK * (r + 1)] = v1[BLK * r : BLK * (r + 1)].T
+    tile = gather(*tile)
+    relay(3)
+    tile = scatter(tile, part_b, got_b, peers_b, sum_send.at[1], sum_recv.at[1])
+    for r in range(8):
+        turned2[:, BLK * r : BLK * (r + 1)] = v2[BLK * r : BLK * (r + 1)].T
+    tile = gather(*tile)
+    grams = [tile[2 * i : 2 * i + 2] for i in range(7)]
     weights = combination(grams[:3], grams[3:6], grams[6])
     weights = jnp.concatenate(list(weights) + [jnp.zeros((BLK - 6, BLK), F32)], axis=0).T
     n_classes = seed.shape[0]
@@ -398,6 +393,7 @@
     turned = pltpu.VMEM((WIDE, 1024), F32)
     code = pltpu.VMEM((24, BLK), F32)
     tile = pltpu.VMEM((8, BLK), F32)
+    sums = pltpu.VMEM((16, BLK), F32)
     outside = pltpu.VMEM((4, WIDE, WIDE), F32)
     return pl.pallas_call(
         functools.partial(kernel, n_rows, n_cls),
@@ -417,20 +413,19 @@
             code, code, code, tile, tile, tile,
             pltpu.VMEM((4, WIDE, WIDE), BF16), pltpu.VMEM((4, WIDE, WIDE), BF16),
             pltpu.VMEM((2, WIDE, WIDE), BF16), pltpu.VMEM((2, WIDE, WIDE), BF16),
-            tile, tile, tile,
-            pltpu.VMEM((GROUP - 1, 8, BLK), F32),
-            pltpu.VMEM((max(n_high - 1, 1), 8, BLK), F32),
-            pltpu.VMEM((n_rows - 1, 8, BLK), F32),
+            sums, sums,
+            pltpu.VMEM((GROUP - 1, 16, BLK), F32),
+            pltpu.VMEM((max(n_high - 1, 1), 16, BLK), F32),
             tile,
             pltpu.VMEM((max(n_cls - 1, 1), 8, BLK), F32),
             pltpu.SemaphoreType.DMA((10,)),
             pltpu.SemaphoreType.DMA((10,)),
             pltpu.SemaphoreType.DMA((10,)),
-            pltpu.SemaphoreType.DMA((3,)),
-            pltpu.SemaphoreType.DMA((3,)),
+            pltpu.SemaphoreType.DMA((2,)),
+            pltpu.SemaphoreType.DMA((2,)),
             pltpu.SemaphoreType.DMA,
             pltpu.SemaphoreType.DMA,
-            pltpu.SemaphoreType.REGULAR((max(n_high // 2, 1),)),
+            pltpu.SemaphoreType.REGULAR((max(n_high // 2 - 1, 1),)),
         ],
         compiler_params=pltpu.CompilerParams(
             collective_id=0, has_side_effects=True, vmem_limit_bytes=VMEM_BYTES

time: 38.4 us -> 32.7 us (0.85)
  the two profiles are of different devices: /device:TPU:1 before, /device:TPU:2 now
where the time goes in v2:
time: 32.7 us; the launch traced here: 32.6 us
  Pallas kernels  31 us (95%)
  local copies, waits for them, and re-layouts  1.66 us (5%)
    pallas_call x1, Pallas kernels, shards(): pl.pallas_call(functools.partial(kernel, n_rows, n_cls), out_shape=jax.Sh...  31 us
    unnamed x3, local copies, waits for them, and re-layouts  1.66 us

profile of v2, /device:TPU:2, one launch (start us, length us, event | category | flops | bytes accessed | tf_op | source)
XLA Modules:
  0.0 32.6 jit_solution(9886239853991550212)
XLA Ops:
  0.0 0.0 copy-start
  0.0 0.7 %copy-done = s32[8,8]{1,0:T(8,128)S(1)} copy-done((s32[8,8]{1,0:T(8,128)S(1)}, s32[8,8]{1,0:T(8,128)}, u32[]{:S(2)}) %copy-start) | copy-done | bytes 280
  0.7 31.0 %shard_map.37 = f32[250,1024]{1,0:T(8,128)S(1)} custom-call(f32[250,1024]{1,0:T(8,128)} %seed_hbm.1, s32[8,8]{1,0:T(8,128)S(1)} %copy-done, bf16[8,8,128,128]{3,2,1,0:T(8,128)(2,1)} %affinity_hbm.1), custom_call_target="tpu_custom_call" | custom-call | flops 1600000000 | bytes 4000000 | tf_op jit(solution)/shard_map/pallas_call | solution.py:398
  31.6 1.0 %copy.5 = f32[250,1024]{1,0:T(8,128)} copy(f32[250,1024]{1,0:T(8,128)S(1)} %shard_map.37) | data formatting | bytes 2048000
Async XLA Ops:
  0.0 0.7 %copy-start = (s32[8,8]{1,0:T(8,128)S(1)}, s32[8,8]{1,0:T(8,128)}, u32[]{:S(2)}) copy-start(s32[8,8]{1,0:T(8,128)} %columns_hbm.1) | copy-start | bytes 772

commit v3 on v2

--- a/solution.py
+++ b/solution.py
@@ -104,7 +104,14 @@
     barrier = pltpu.get_barrier_semaphore()
     above = {"rows": lax.rem(high + 1, n_high) * GROUP + low, "cls": mine}
     below = {"rows": lax.rem(high + n_high - 1, n_high) * GROUP + low, "cls": mine}
-    partners = [left, right] + [above, below] + peers_a + peers_c
+    core = lax.rem(low, 2)
+    beside = [
+        {"rows": high * GROUP + lax.rem(low + step, GROUP), "cls": mine} for step in (2, GROUP - 2)
+    ] + [{"rows": me, "cls": lax.rem(mine + step, n_cls)} for step in (1, n_cls - 1)] + [above, below]
+    crossed = [
+        {"rows": high * GROUP + lax.rem(low + 1 - 2 * core + step, GROUP), "cls": mine} for step in (GROUP, GROUP + 2, GROUP - 2)
+    ]
+    partners = [left, right] + beside + crossed
     for device in partners:
         pl.semaphore_signal(barrier, inc=1, device_id=device, device_id_type=MESH)
 
@@ -144,13 +151,13 @@
 
     scattered = []
 
-    n_relays = max(n_high // 2 - 1, 0)
+    n_relays = max(n_high // 2 - 1, 1)
 
     def relay(step):
         if 0 < step <= n_relays:
-            pl.semaphore_wait(relay_sem.at[step - 1], 2)
+            pl.semaphore_wait(relay_sem.at[step - 1], len(beside) if step == 1 else 2)
         if step < n_relays:
-            for device in (above, below):
+            for device in beside if step == 0 else (above, below):
                 pl.semaphore_signal(relay_sem.at[step], inc=1, device_id=device, device_id_type=MESH)
 
     lane = lax.broadcasted_iota(jnp.int32, (BLK, BLK), 1)
@@ -186,9 +193,10 @@
             column(code, 8 + r, WIDE) == wide_lane, column(code, r, WIDE), 0.0
         )
 
+    for copy in raw_copies:
+        copy.wait()
     inverses = jnp.zeros((BLK, BLK), F32)
     for r in range(8):
-        raw_copies[r].wait()
         degree = jnp.sum(jnp.sum(raw[r].astype(F32), axis=0), axis=1, keepdims=True)
         inverse = lax.rsqrt(degree)
         root[BLK * r : BLK * (r + 1)] = jnp.broadcast_to(inverse, (BLK, WIDE))

time: 32.7 us -> 32.5 us (level)
  no operation moved by 1% of the time
where the time goes in v3:
time: 32.5 us; the launch traced here: 32.4 us
  Pallas kernels  30.7 us (94%)
  local copies, waits for them, and re-layouts  1.66 us (5%)
    pallas_call x1, Pallas kernels, shards(): pl.pallas_call(functools.partial(kernel, n_rows, n_cls), out_shape=jax.Sh...  30.7 us
    unnamed x3, local copies, waits for them, and re-layouts  1.66 us

profile of v3, /device:TPU:2, one launch (start us, length us, event | category | flops | bytes accessed | tf_op | source)
XLA Modules:
  0.0 32.4 jit_solution(7730647687866587883)
XLA Ops:
  0.0 0.0 copy-start
  0.0 0.7 %copy-done = s32[8,8]{1,0:T(8,128)S(1)} copy-done((s32[8,8]{1,0:T(8,128)S(1)}, s32[8,8]{1,0:T(8,128)}, u32[]{:S(2)}) %copy-start) | copy-done | bytes 280
  0.7 30.7 %shard_map.37 = f32[250,1024]{1,0:T(8,128)S(1)} custom-call(f32[250,1024]{1,0:T(8,128)} %seed_hbm.1, s32[8,8]{1,0:T(8,128)S(1)} %copy-done, bf16[8,8,128,128]{3,2,1,0:T(8,128)(2,1)} %affinity_hbm.1), custom_call_target="tpu_custom_call" | custom-call | flops 1600000000 | bytes 4000000 | tf_op jit(solution)/shard_map/pallas_call | solution.py:406
  31.4 1.0 %copy.5 = f32[250,1024]{1,0:T(8,128)} copy(f32[250,1024]{1,0:T(8,128)S(1)} %shard_map.37) | data formatting | bytes 2048000
Async XLA Ops:
  0.0 0.7 %copy-start = (s32[8,8]{1,0:T(8,128)S(1)}, s32[8,8]{1,0:T(8,128)}, u32[]{:S(2)}) copy-start(s32[8,8]{1,0:T(8,128)} %columns_hbm.1) | copy-start | bytes 772

commit v4 on v3

--- a/solution.py
+++ b/solution.py
@@ -71,7 +71,7 @@
 
 def kernel(
     n_rows, n_cls,
-    seed_hbm, columns_hbm, affinity_hbm, result,
+    seed_hbm, columns_hbm, affinity_hbm, result, norm_out,
     columns_ref, seed, raw, band, across, field1, field2a, field2b, field3a, field3b, v0, v1, v2, root, self_part, outer_root, outer_v0, outer_self,
     reach, turned1, turned2,
     code_out, code_left, code_right, apart_out, apart_left, apart_right, first_out, first_in, second_out, second_in,
@@ -84,21 +84,18 @@
     n_high = n_rows // GROUP
     total_blocks = n_rows * 8
 
-    columns_copy = pltpu.make_async_copy(columns_hbm, columns_ref, load_sem.at[9])
+    columns_copy = pltpu.make_async_copy(columns_hbm, columns_ref, load_sem.at[1])
     columns_copy.start()
-    seed_copy = pltpu.make_async_copy(seed_hbm, seed, load_sem.at[8])
+    seed_copy = pltpu.make_async_copy(seed_hbm, seed, load_sem.at[2])
     seed_copy.start()
-    raw_copies = []
-    for r in range(8):
-        copy = pltpu.make_async_copy(affinity_hbm.at[r], raw.at[r], load_sem.at[r])
-        copy.start()
-        raw_copies.append(copy)
+    raw_copy = pltpu.make_async_copy(affinity_hbm, raw, load_sem.at[0])
+    raw_copy.start()
 
     left = {"rows": lax.rem(me + n_rows - 1, n_rows), "cls": mine}
     right = {"rows": lax.rem(me + 1, n_rows), "cls": mine}
     far = sorted(range(1, GROUP), key=lambda d: -min(d, GROUP - d))
     peers_a = [{"rows": high * GROUP + lax.rem(low + d, GROUP), "cls": mine} for d in far]
-    peers_b = [{"rows": lax.rem(high + d, n_high) * GROUP + low, "cls": mine} for d in range(1, n_high)]
+    peers_b = [{"rows": lax.rem(high + d, n_high) * GROUP + low, "cls": mine} for d in sorted(range(1, n_high), key=lambda d: (d > n_high // 2, -d if d <= n_high // 2 else d))]
     far = sorted(range(1, n_cls), key=lambda d: -min(d, n_cls - d))
     peers_c = [{"rows": me, "cls": lax.rem(mine + d, n_cls)} for d in far]
     barrier = pltpu.get_barrier_semaphore()
@@ -193,8 +190,7 @@
             column(code, 8 + r, WIDE) == wide_lane, column(code, r, WIDE), 0.0
         )
 
-    for copy in raw_copies:
-        copy.wait()
+    raw_copy.wait()
     inverses = jnp.zeros((BLK, BLK), F32)
     for r in range(8):
         degree = jnp.sum(jnp.sum(raw[r].astype(F32), axis=0), axis=1, keepdims=True)
@@ -384,9 +380,7 @@
     strength = jnp.concatenate([strength[:, BLK * r : BLK * (r + 1)] for r in range(8)], axis=0)
     strength = gather(*scatter(strength, strength_out, strength_in, peers_c, cls_send, cls_recv))
     norm = lax.rsqrt(strength + epsilon)
-    for r in range(8):
-        here = pl.ds(BLK * r, BLK)
-        result[:, here] = result[:, here] * norm[r : r + 1]
+    norm_out[...] = jnp.concatenate([norm[r : r + 1] for r in range(8)], axis=1)
     for copy in sent:
         copy.wait_send()
     for got, send_sem in scattered:
@@ -403,11 +397,11 @@
     tile = pltpu.VMEM((8, BLK), F32)
     sums = pltpu.VMEM((16, BLK), F32)
     outside = pltpu.VMEM((4, WIDE, WIDE), F32)
-    return pl.pallas_call(
+    x, norm = pl.pallas_call(
         functools.partial(kernel, n_rows, n_cls),
-        out_shape=jax.ShapeDtypeStruct(seed_scores.shape, F32),
+        out_shape=(jax.ShapeDtypeStruct(seed_scores.shape, F32), jax.ShapeDtypeStruct((1, n_nodes), F32)),
         in_specs=[pl.BlockSpec(memory_space=pl.ANY)] * 3,
-        out_specs=pl.BlockSpec(memory_space=pltpu.VMEM),
+        out_specs=(pl.BlockSpec(memory_space=pltpu.VMEM), pl.BlockSpec(memory_space=pltpu.VMEM)),
         scratch_shapes=[
             pltpu.SMEM((8, NNZB), jnp.int32),
             pltpu.VMEM((n_classes, n_nodes), F32),
@@ -426,7 +420,7 @@
             pltpu.VMEM((max(n_high - 1, 1), 16, BLK), F32),
             tile,
             pltpu.VMEM((max(n_cls - 1, 1), 8, BLK), F32),
-            pltpu.SemaphoreType.DMA((10,)),
+            pltpu.SemaphoreType.DMA((3,)),
             pltpu.SemaphoreType.DMA((10,)),
             pltpu.SemaphoreType.DMA((10,)),
             pltpu.SemaphoreType.DMA((2,)),
@@ -440,6 +434,7 @@
         ),
         cost_estimate=pl.CostEstimate(flops=1600000000, bytes_accessed=4000000, transcendentals=0),
     )(seed_scores, block_columns, affinity)
+    return x * norm
 
 
 def solution(mesh):

time: 32.5 us -> 32.1 us (0.988)
  other arithmetic: 0 us -> 1.09 us
  local copies, waits for them, and re-layouts: 1.66 us -> 0.69 us
  Pallas kernels: 30.7 us -> 30.2 us
    mul x0 -> x1, other arithmetic: none -> 1.09 us  [shards(): return x * norm]
    unnamed x3 -> x2, local copies, waits for them, and re-layouts: 1.66 us -> 0.69 us
    pallas_call x1, Pallas kernels: 30.7 us -> 30.2 us  [shards(): pl.pallas_call(functools.partial(kernel, n_rows, n_cls), out_shape=(jax.S...]
where the time goes in v4:
time: 32.1 us; the launch traced here: 32 us
  Pallas kernels  30.2 us (94%)
  other arithmetic  1.09 us (3%)
  local copies, waits for them, and re-layouts  0.69 us (2%)
    pallas_call x1, Pallas kernels, shards(): pl.pallas_call(functools.partial(kernel, n_rows, n_cls), out_shape=(jax.S...  30.2 us
    mul x1, other arithmetic, shards(): return x * norm  1.09 us
    unnamed x2, local copies, waits for them, and re-layouts  0.69 us

profile of v4, /device:TPU:2, one launch (start us, length us, event | category | flops | bytes accessed | tf_op | source)
XLA Modules:
  0.0 32.0 jit_solution(5314305133089619686)
XLA Ops:
  0.0 0.0 copy-start
  0.0 0.7 %copy-done = s32[8,8]{1,0:T(8,128)S(1)} copy-done((s32[8,8]{1,0:T(8,128)S(1)}, s32[8,8]{1,0:T(8,128)}, u32[]{:S(2)}) %copy-start) | copy-done | bytes 280
  0.7 30.2 %shard_map.37 = (f32[250,1024]{1,0:T(8,128)S(1)}, f32[1,1024]{1,0:T(1,128)S(1)}) custom-call(f32[250,1024]{1,0:T(8,128)} %seed_hbm.1, s32[8,8]{1,0:T(8,128)S(1)} %copy-done, bf16[8,8,128,128]{3,2,1,0:T(8,128)(2,1)} %affinity_hbm.1), custom_call_target="tpu_custom_call" | custom-call | flops 1600000000 | bytes 4000000 | tf_op jit(solution)/shard_map/pallas_call | solution.py:400
  30.9 1.1 %broadcast_multiply_fusion = f32[250,1024]{1,0:T(8,128)} fusion(f32[250,1024]{1,0:T(8,128)S(1)} %get-tuple-element.7, f32[1024]{0:T(1024)S(1)} %bitcast.1), kind=kLoop, calls=%fused_computation | loop fusion | flops 256000 | bytes 2052096 | tf_op jit(solution)/shard_map/mul | solution.py:437
Async XLA Ops:
  0.0 0.7 %copy-start = (s32[8,8]{1,0:T(8,128)S(1)}, s32[8,8]{1,0:T(8,128)}, u32[]{:S(2)}) copy-start(s32[8,8]{1,0:T(8,128)} %columns_hbm.1) | copy-start | bytes 772

commit v5 on v4

--- a/solution.py
+++ b/solution.py
@@ -335,7 +335,9 @@
     form = jnp.zeros((1, WIDE), F32)
     for i in range(4):
         field = pair(v2, i)[...]
-        form = form + node_sum(field * (own(field3, i) + pair(self_part, i)[...] * field))
+        high_part = field3a[512 + WIDE * i : 512 + WIDE * (i + 1)].astype(F32)
+        either = 2.0 * pair(root, i)[...] * field - high_part
+        form = form + node_sum(either * part(i, (field3a,), OWN[i]) + pair(self_part, i)[...] * field * field)
     for n, (h, k, pairs) in enumerate(((1, 1, (1,)), (2, 6, (2, 3)))):
         inverse = outer_root[h]
         weight = 2.0 * inverse * outward(field3, k, pairs)

time: 32.1 us -> 32.1 us (level)
  no operation moved by 1% of the time
where the time goes in v5:
time: 32.1 us; the launch traced here: 32 us
  Pallas kernels  30.2 us (94%)
  other arithmetic  1.09 us (3%)
  local copies, waits for them, and re-layouts  0.69 us (2%)
    pallas_call x1, Pallas kernels, shards(): pl.pallas_call(functools.partial(kernel, n_rows, n_cls), out_shape=(jax.S...  30.2 us
    mul x1, other arithmetic, shards(): return x * norm  1.09 us
    unnamed x2, local copies, waits for them, and re-layouts  0.69 us

profile of v5, /device:TPU:2, one launch (start us, length us, event | category | flops | bytes accessed | tf_op | source)
XLA Modules:
  0.0 32.0 jit_solution(2992826249926417382)
XLA Ops:
  0.0 0.0 copy-start
  0.0 0.7 %copy-done = s32[8,8]{1,0:T(8,128)S(1)} copy-done((s32[8,8]{1,0:T(8,128)S(1)}, s32[8,8]{1,0:T(8,128)}, u32[]{:S(2)}) %copy-start) | copy-done | bytes 280
  0.7 30.2 %shard_map.37 = (f32[250,1024]{1,0:T(8,128)S(1)}, f32[1,1024]{1,0:T(1,128)S(1)}) custom-call(f32[250,1024]{1,0:T(8,128)} %seed_hbm.1, s32[8,8]{1,0:T(8,128)S(1)} %copy-done, bf16[8,8,128,128]{3,2,1,0:T(8,128)(2,1)} %affinity_hbm.1), custom_call_target="tpu_custom_call" | custom-call | flops 1600000000 | bytes 4000000 | tf_op jit(solution)/shard_map/pallas_call | solution.py:402
  30.9 1.1 %broadcast_multiply_fusion = f32[250,1024]{1,0:T(8,128)} fusion(f32[250,1024]{1,0:T(8,128)S(1)} %get-tuple-element.7, f32[1024]{0:T(1024)S(1)} %bitcast.1), kind=kLoop, calls=%fused_computation | loop fusion | flops 256000 | bytes 2052096 | tf_op jit(solution)/shard_map/mul | solution.py:439
Async XLA Ops:
  0.0 0.7 %copy-start = (s32[8,8]{1,0:T(8,128)S(1)}, s32[8,8]{1,0:T(8,128)}, u32[]{:S(2)}) copy-start(s32[8,8]{1,0:T(8,128)} %columns_hbm.1) | copy-start | bytes 772

commit v6 on v4

--- a/solution.py
+++ b/solution.py
@@ -83,13 +83,6 @@
     low, high = lax.rem(me, GROUP), me // GROUP
     n_high = n_rows // GROUP
     total_blocks = n_rows * 8
-
-    columns_copy = pltpu.make_async_copy(columns_hbm, columns_ref, load_sem.at[1])
-    columns_copy.start()
-    seed_copy = pltpu.make_async_copy(seed_hbm, seed, load_sem.at[2])
-    seed_copy.start()
-    raw_copy = pltpu.make_async_copy(affinity_hbm, raw, load_sem.at[0])
-    raw_copy.start()
 
     left = {"rows": lax.rem(me + n_rows - 1, n_rows), "cls": mine}
     right = {"rows": lax.rem(me + 1, n_rows), "cls": mine}
@@ -111,6 +104,13 @@
     partners = [left, right] + beside + crossed
     for device in partners:
         pl.semaphore_signal(barrier, inc=1, device_id=device, device_id_type=MESH)
+
+    columns_copy = pltpu.make_async_copy(columns_hbm, columns_ref, load_sem.at[1])
+    columns_copy.start()
+    seed_copy = pltpu.make_async_copy(seed_hbm, seed, load_sem.at[2])
+    seed_copy.start()
+    raw_copy = pltpu.make_async_copy(affinity_hbm, raw, load_sem.at[0])
+    raw_copy.start()
 
     sent = []
 

time: 32.1 us -> 32.1 us (level)
  no operation moved by 1% of the time
where the time goes in v6:
time: 32.1 us; the launch traced here: 32 us
  Pallas kernels  30.2 us (94%)
  other arithmetic  1.09 us (3%)
  local copies, waits for them, and re-layouts  0.69 us (2%)
    pallas_call x1, Pallas kernels, shards(): pl.pallas_call(functools.partial(kernel, n_rows, n_cls), out_shape=(jax.S...  30.2 us
    mul x1, other arithmetic, shards(): return x * norm  1.09 us
    unnamed x2, local copies, waits for them, and re-layouts  0.69 us

profile of v6, /device:TPU:2, one launch (start us, length us, event | category | flops | bytes accessed | tf_op | source)
XLA Modules:
  0.0 32.0 jit_solution(11552599877124718875)
XLA Ops:
  0.0 0.0 copy-start
  0.0 0.7 %copy-done = s32[8,8]{1,0:T(8,128)S(1)} copy-done((s32[8,8]{1,0:T(8,128)S(1)}, s32[8,8]{1,0:T(8,128)}, u32[]{:S(2)}) %copy-start) | copy-done | bytes 280
  0.7 30.2 %shard_map.37 = (f32[250,1024]{1,0:T(8,128)S(1)}, f32[1,1024]{1,0:T(1,128)S(1)}) custom-call(f32[250,1024]{1,0:T(8,128)} %seed_hbm.1, s32[8,8]{1,0:T(8,128)S(1)} %copy-done, bf16[8,8,128,128]{3,2,1,0:T(8,128)(2,1)} %affinity_hbm.1), custom_call_target="tpu_custom_call" | custom-call | flops 1600000000 | bytes 4000000 | tf_op jit(solution)/shard_map/pallas_call | solution.py:400
  30.9 1.1 %broadcast_multiply_fusion = f32[250,1024]{1,0:T(8,128)} fusion(f32[250,1024]{1,0:T(8,128)S(1)} %get-tuple-element.7, f32[1024]{0:T(1024)S(1)} %bitcast.1), kind=kLoop, calls=%fused_computation | loop fusion | flops 256000 | bytes 2052096 | tf_op jit(solution)/shard_map/mul | solution.py:437
Async XLA Ops:
  0.0 0.7 %copy-start = (s32[8,8]{1,0:T(8,128)S(1)}, s32[8,8]{1,0:T(8,128)}, u32[]{:S(2)}) copy-start(s32[8,8]{1,0:T(8,128)} %columns_hbm.1) | copy-start | bytes 772
